TPU v7x, 32 devices: a whole 2x2x4 slice. The times are simulated.
32 devices in a mesh: rows: 4 (over z), cols: 4 (over y, core), rep: 2 (over x).
Axes of the slice: x: 2, y: 2, z: 4, core: 2. Of those that a mesh axis runs over, the one named last changes fastest.
Arguments:
- inputs: bfloat16 [8, 64, 128, 256], P('rep', 'rows', 'cols'), may hold values from -6 to 6
- upstream: bfloat16 [8, 64, 128, 256], P('rep', 'rows', 'cols'), may hold values from -6 to 6
- kernel: bfloat16 [3, 3, 256, 256], replicated, may hold values from -0.125 to 0.125
- probe_init: float32 [64, 128, 256], P('rows', 'cols'), may hold values from -18 to 18
Outputs:
- outputs: bfloat16 [8, 64, 128, 256], P('rep', 'rows', 'cols')
- input_grad: bfloat16 [8, 64, 128, 256], P('rep', 'rows', 'cols')
- kernel_grad: float32 [256, 2304], P(('rows', 'cols'))
- probe_out: float32 [64, 128, 256], P('rows', 'cols')
- lipschitz: float32 [], replicated
- norm_trace: float32 [3], replicated
All inputs are finite; a program needn't handle non-finite values.
Results may differ from a plain program's by a relative error of at most 0.011.
Values may be sent and summed in bfloat16 or wider, within the bound.
A program may use at most 128 MiB of HBM per device.

v0:
```python
import math

import jax
import jax.numpy as jnp
from jax import lax
from jax.sharding import PartitionSpec as P

ITERS = 4


def extended(cells, sides, width, closed):
    for axis, dim in sides:
        count = lax.axis_size(axis)
        ends = count if closed else count - 1
        head = lax.slice_in_dim(cells, 0, width, axis=dim)
        tail = lax.slice_in_dim(cells, cells.shape[dim] - width, cells.shape[dim], axis=dim)
        cells = jnp.concatenate(
            [
                lax.ppermute(tail, axis, [(i, (i + 1) % count) for i in range(ends)]),
                cells,
                lax.ppermute(head, axis, [((i + 1) % count, i) for i in range(ends)]),
            ],
            axis=dim,
        )
    return cells


def tap_sum(padded, kernel, height, breadth, adjoint):
    summed = None
    for row_tap in range(3):
        for col_tap in range(3):
            if adjoint:
                window = padded[
                    ..., 2 - row_tap : 2 - row_tap + height, 2 - col_tap : 2 - col_tap + breadth, :
                ]
                contrib = jnp.einsum(
                    "...d,cd->...c",
                    window,
                    kernel[row_tap, col_tap],
                    preferred_element_type=jnp.float32,
                )
            else:
                window = padded[..., row_tap : row_tap + height, col_tap : col_tap + breadth, :]
                contrib = jnp.einsum(
                    "...c,cd->...d",
                    window,
                    kernel[row_tap, col_tap],
                    preferred_element_type=jnp.float32,
                )
            summed = contrib if summed is None else summed + contrib
    return summed


def per_device(inputs, upstream, kernel, probe_init):
    height = inputs.shape[1]
    breadth = inputs.shape[2]
    channels = kernel.shape[2]
    rows_count = lax.axis_size("rows")
    cols_count = lax.axis_size("cols")
    count = float(height * rows_count * breadth * cols_count * channels)
    iterate = probe_init.astype(jnp.bfloat16)
    back = None
    traces = []
    local_sums = []
    for iteration in range(ITERS):
        padded_probe = extended(iterate, (("rows", 0), ("cols", 1)), 1, True)
        image = tap_sum(padded_probe, kernel, height, breadth, False).astype(jnp.bfloat16)
        padded_image = extended(image, (("rows", 0), ("cols", 1)), 1, True)
        back = tap_sum(padded_image, kernel, height, breadth, True)
        if iteration + 1 < ITERS:
            squared = lax.psum(jnp.sum(back * back), ("rows", "cols"))
            scale_now = jnp.sqrt(squared / count + 1e-06)
            traces.append(scale_now)
            iterate = (back / scale_now).astype(jnp.bfloat16)
    wide_iter = iterate.astype(jnp.float32)
    totals = lax.psum(
        jnp.stack([jnp.sum(back * back), jnp.sum(wide_iter * wide_iter)] + local_sums),
        ("rows", "cols"),
    )
    sum_back = totals[0]
    sum_probe = totals[1]
    norm_trace = jnp.stack(traces)
    lipschitz = jnp.sqrt(jnp.sqrt(sum_back / sum_probe))
    probe_out = back / jnp.sqrt(sum_back / count + 1e-06)
    padded_in = extended(inputs, (("rows", 1), ("cols", 2)), 1, False)
    outputs = tap_sum(padded_in, kernel, height, breadth, False).astype(jnp.bfloat16)
    padded_up = extended(upstream, (("rows", 1), ("cols", 2)), 1, False)
    input_grad = tap_sum(padded_up, kernel, height, breadth, True).astype(jnp.bfloat16)
    pieces = []
    for row_tap in range(3):
        for col_tap in range(3):
            window = padded_in[:, row_tap : row_tap + height, col_tap : col_tap + breadth, :]
            pieces.append(
                jnp.einsum("nhwd,nhwc->dc", upstream, window, preferred_element_type=jnp.float32)
            )
    local_grad = jnp.stack(pieces, axis=1).reshape(channels, 9 * channels)
    replica_total = lax.psum(local_grad.astype(jnp.bfloat16), "rep").astype(jnp.float32)
    owned = lax.psum_scatter(replica_total, ("rows", "cols"), scatter_dimension=0, tiled=True)
    total_cells = (
        inputs.shape[0] * lax.axis_size("rep") * height * rows_count * breadth * cols_count
    )
    kernel_grad = owned * (1.0 / math.sqrt(total_cells))
    return (outputs, input_grad, kernel_grad, probe_out, lipschitz, norm_trace)


def solution(mesh):
    placed = (
        P("rep", "rows", "cols", None),
        P("rep", "rows", "cols", None),
        P(),
        P("rows", "cols", None),
    )
    return jax.shard_map(
        per_device,
        mesh=mesh,
        in_specs=placed,
        out_specs=(
            P("rep", "rows", "cols", None),
            P("rep", "rows", "cols", None),
            P(("rows", "cols"), None),
            P("rows", "cols", None),
            P(),
            P(),
        ),
        check_vma=False,
    )
```

profile of v0, /device:TPU:0, one launch (start us, length us, event | category | flops | bytes accessed | tf_op | source)
XLA Modules:
  0.0 342.4 jit_solution(11548452925381940797)
XLA Ops:
  8.4 3.1 collective-permute-start.8
  11.5 2.1 collective-permute-start.9
  19.8 4.7 %collective-permute-start.4 = (bf16[4,1,32,256]{3,2,1,0:T(8,128)(2,1)}, bf16[4,1,32,256]{3,2,1,0:T(8,128)(2,1)S(1)}, u32[]{:S(2)}, u32[]{:S(2)}) collective-permute-start(bf16[4,1,32,256]{3,2,1,0:T(8,128)(2,1)} %get-tuple-element.22), channel_id=1, source_target_pairs={{0,8},{8,16},{16,24},{1,9},{9,17},{17,25},{2,10},{10,18},{18,26},{... | collective-permute-start | bytes 196616 | tf_op jit(solution)/shard_map/ppermute | solution.py:19
  24.4 3.0 fusion.356
  36.2 2.2 collective-permute-start.13
  47.3 34.3 %psum.36 = f32[]{:T(128)} all-reduce(f32[]{:T(128)} %get-tuple-element.82), channel_id=1, replica_groups=mesh['rows'=4,'cols'=4,'rep'=2] {'rows','cols'}, use_global_device_ids=true, to_apply=%region_3.0 | all-reduce | flops 1 | bytes 8 | tf_op jit(solution)/shard_map/psum | solution.py:71
  83.7 3.8 %collective-permute-start.17 = (bf16[1,32,256]{2,1,0:T(8,128)(2,1)S(1)}, bf16[1,32,256]{2,1,0:T(8,128)(2,1)S(1)}, u32[]{:S(2)}, u32[]{:S(2)}) collective-permute-start(bf16[1,32,256]{2,1,0:T(8,128)(2,1)S(1)} %get-tuple-element.71), channel_id=1, source_target_pairs={{8,0},{16,8},{24,16},{0,24},{9,1},{17,9},{25,17},{1,25},{10,2},{18... | collective-permute-start | bytes 49160 | tf_op jit(solution)/shard_map/ppermute | solution.py:21
  96.4 2.7 fusion.79
  107.0 2.0 collective-permute-start.20
  114.7 4.6 %collective-permute-start.7 = (bf16[4,18,1,256]{3,2,1,0:T(2,128)(2,1)}, bf16[4,18,1,256]{3,2,1,0:T(2,128)(2,1)S(1)}, u32[]{:S(2)}, u32[]{:S(2)}) collective-permute-start(bf16[4,18,1,256]{3,2,1,0:T(2,128)(2,1)} %get-tuple-element.14), channel_id=1, source_target_pairs={{0,2},{2,4},{4,6},{1,3},{3,5},{5,7},{8,10},{10,12},{12,14},{9,11},... | collective-permute-start | bytes 110600 | tf_op jit(solution)/shard_map/ppermute | solution.py:19
  120.6 4.9 %pad_maximum_fusion.6 = (bf16[4,16,32,256]{3,2,1,0:T(8,128)(2,1)}, bf16[4,16,32,256]{3,2,1,0:T(8,128)(2,1)}, bf16[4,16,32,256]{3,2,1,0:T(8,128)(2,1)}, bf16[4,16...) fusion(bf16[4,18,1,256]{3,2,1,0:T(2,128)(2,1)S(1)} %collective-permute-done.3, ...), kind=kLoop, calls=%fused_computation.148 | loop fusion | flops 12582912 | bytes 7544832 | tf_op jit(solution)/shard_map/concatenate | solution.py:17
  130.4 30.1 %psum.37 = f32[]{:T(128)} all-reduce(f32[]{:T(128)} %get-tuple-element.84), channel_id=1, replica_groups=mesh['rows'=4,'cols'=4,'rep'=2] {'rows','cols'}, use_global_device_ids=true, to_apply=%region_5.0 | all-reduce | flops 1 | bytes 8 | tf_op jit(solution)/shard_map/psum | solution.py:71
  163.6 3.8 %collective-permute-start.25 = (bf16[1,32,256]{2,1,0:T(8,128)(2,1)}, bf16[1,32,256]{2,1,0:T(8,128)(2,1)}, u32[]{:S(2)}, u32[]{:S(2)}) collective-permute-start(bf16[1,32,256]{2,1,0:T(8,128)(2,1)} %get-tuple-element.67), channel_id=1, source_target_pairs={{8,0},{16,8},{24,16},{0,24},{9,1},{17,9},{25,17},{1,25},{10,2},{18... | collective-permute-start | bytes 49160 | tf_op jit(solution)/shard_map/ppermute | solution.py:21
  167.4 2.4 fusion.76
  185.3 2.4 copy.28
  189.0 8.1 %add_convert_fusion.1 = bf16[4,16,32,256]{3,2,1,0:T(8,128)(2,1)} fusion(f32[4,16,32,256]{3,2,1,0:T(8,128)} %fusion.346, f32[4,16,32,256]{3,2,1,0:T(8,128)} %fusion.349, f32[4,16,32,256]{3,2,1,0:T(8,128)} %fusion.352, f32[4,16,32,256]{3,2,1,0:T(8,128)} %fusion.356, f32[4,16,32,256]{3,2,1,0:T(8,128)} %fusion.359, f32[4,16,32,256]{3,2,1,0:T(8,128)} %fusion.362, ...), kind=kOutput, calls=%fused_computation.1 | convolution fusion | flops 273154048 | bytes 19005440 | tf_op jit(solution)/shard_map/...c,cd->...d/dot_general | solution.py:44
  201.6 2.1 add_convert_fusion
  222.5 30.1 %psum.38 = f32[]{:T(128)} all-reduce(f32[]{:T(128)} %get-tuple-element.86), channel_id=1, replica_groups=mesh['rows'=4,'cols'=4,'rep'=2] {'rows','cols'}, use_global_device_ids=true, to_apply=%region_7.0 | all-reduce | flops 1 | bytes 8 | tf_op jit(solution)/shard_map/psum | solution.py:71
  254.1 3.8 %collective-permute-start.33 = (bf16[1,32,256]{2,1,0:T(8,128)(2,1)S(1)}, bf16[1,32,256]{2,1,0:T(8,128)(2,1)S(1)}, u32[]{:S(2)}, u32[]{:S(2)}) collective-permute-start(bf16[1,32,256]{2,1,0:T(8,128)(2,1)S(1)} %get-tuple-element.63), channel_id=1, source_target_pairs={{8,0},{16,8},{24,16},{0,24},{9,1},{17,9},{25,17},{1,25},{10,2},{18... | collective-permute-start | bytes 49160 | tf_op jit(solution)/shard_map/ppermute | solution.py:21
  265.1 2.8 convert_element_type.43
  269.3 3.9 %collective-permute-start.37 = (bf16[1,32,256]{2,1,0:T(8,128)(2,1)S(1)}, bf16[1,32,256]{2,1,0:T(8,128)(2,1)S(1)}, u32[]{:S(2)}, u32[]{:S(2)}) collective-permute-start(bf16[1,32,256]{2,1,0:T(8,128)(2,1)S(1)} %get-tuple-element.61), channel_id=1, source_target_pairs={{8,0},{16,8},{24,16},{0,24},{9,1},{17,9},{25,17},{1,25},{10,2},{18... | collective-permute-start | bytes 49160 | tf_op jit(solution)/shard_map/ppermute | solution.py:21
  274.6 4.1 %collective-permute-done.36 = bf16[1,32,256]{2,1,0:T(8,128)(2,1)S(1)} collective-permute-done((bf16[1,32,256]{2,1,0:T(8,128)(2,1)S(1)}, bf16[1,32,256]{2,1,0:T(8,128)(2,1)S(1)}, u32[]{:S(2)}, u32[]{:S(2)}) %collective-permute-start.36) | collective-permute-done | bytes 16416 | tf_op jit(solution)/shard_map/ppermute | solution.py:19
  286.8 29.9 %psum.39 = f32[2]{0:T(128)S(1)} all-reduce(f32[2]{0:T(128)S(1)} %pad_maximum_fusion.40), channel_id=1, replica_groups=mesh['rows'=4,'cols'=4,'rep'=2] {'rows','cols'}, use_global_device_ids=true, to_apply=%region_10.0 | all-reduce | flops 2 | bytes 16 | tf_op jit(solution)/shard_map/psum | solution.py:76
  320.2 12.6 %reduce-scatter.2.cloned.1.call-done = f32[16,2304]{1,0:T(8,128)} async-done(((f32[256,2304]{1,0:T(8,128)}), f32[16,2304]{1,0:T(8,128)}) %reduce-scatter.2.cloned.1.call-update) | async-done | bytes 147472 | tf_op jit(solution)/shard_map/reduce_scatter | solution.py:98
  (249 shorter events, 118.5 us)
Async XLA Ops:
  7.2 257.9 %all-reduce.2.cloned.1.call-start = ((), (), s32[]{:S(2)}) async-start(), calls=%async_computation.1 | async-start | bytes 2359296 | tf_op jit(solution)/shard_map/psum | solution.py:97
  8.4 21.1 %collective-permute-start.8 = (bf16[1,32,256]{2,1,0:T(8,128)(2,1)S(1)}, bf16[1,32,256]{2,1,0:T(8,128)(2,1)S(1)}, u32[]{:S(2)}, u32[]{:S(2)}) collective-permute-start(bf16[1,32,256]{2,1,0:T(8,128)(2,1)S(1)} %get-tuple-element.74), channel_id=1, source_target_pairs={{0,8},{8,16},{16,24},{24,0},{1,9},{9,17},{17,25},{25,1},{2,10},{10... | collective-permute-start | bytes 49160 | tf_op jit(solution)/shard_map/ppermute | solution.py:19
  11.5 18.1 %collective-permute-start.9 = (bf16[1,32,256]{2,1,0:T(8,128)(2,1)S(1)}, bf16[1,32,256]{2,1,0:T(8,128)(2,1)S(1)}, u32[]{:S(2)}, u32[]{:S(2)}) collective-permute-start(bf16[1,32,256]{2,1,0:T(8,128)(2,1)S(1)} %get-tuple-element.75), channel_id=1, source_target_pairs={{8,0},{16,8},{24,16},{0,24},{9,1},{17,9},{25,17},{1,25},{10,2},{18... | collective-permute-start | bytes 49160 | tf_op jit(solution)/shard_map/ppermute | solution.py:21
  15.1 68.6 %collective-permute-start = (bf16[4,1,32,256]{3,2,1,0:T(8,128)(2,1)}, bf16[4,1,32,256]{3,2,1,0:T(8,128)(2,1)S(1)}, u32[]{:S(2)}, u32[]{:S(2)}) collective-permute-start(bf16[4,1,32,256]{3,2,1,0:T(8,128)(2,1)} %get-tuple-element.26), channel_id=1, source_target_pairs={{0,8},{8,16},{16,24},{1,9},{9,17},{17,25},{2,10},{10,18},{18,26},{... | collective-permute-start | bytes 196616 | tf_op jit(solution)/shard_map/ppermute | solution.py:19
  16.9 70.9 %collective-permute-start.1 = (bf16[4,1,32,256]{3,2,1,0:T(8,128)(2,1)}, bf16[4,1,32,256]{3,2,1,0:T(8,128)(2,1)S(1)}, u32[]{:S(2)}, u32[]{:S(2)}) collective-permute-start(bf16[4,1,32,256]{3,2,1,0:T(8,128)(2,1)} %get-tuple-element.27), channel_id=1, source_target_pairs={{8,0},{16,8},{24,16},{9,1},{17,9},{25,17},{10,2},{18,10},{26,18},{... | collective-permute-start | bytes 196616 | tf_op jit(solution)/shard_map/ppermute | solution.py:21
  19.8 73.2 %collective-permute-start.4 = (bf16[4,1,32,256]{3,2,1,0:T(8,128)(2,1)}, bf16[4,1,32,256]{3,2,1,0:T(8,128)(2,1)S(1)}, u32[]{:S(2)}, u32[]{:S(2)}) collective-permute-start(bf16[4,1,32,256]{3,2,1,0:T(8,128)(2,1)} %get-tuple-element.22), channel_id=1, source_target_pairs={{0,8},{8,16},{16,24},{1,9},{9,17},{17,25},{2,10},{10,18},{18,26},{... | collective-permute-start | bytes 196616 | tf_op jit(solution)/shard_map/ppermute | solution.py:19
  34.5 5.6 %collective-permute-start.12 = (bf16[1,32,256]{2,1,0:T(8,128)(2,1)S(1)}, bf16[1,32,256]{2,1,0:T(8,128)(2,1)S(1)}, u32[]{:S(2)}, u32[]{:S(2)}) collective-permute-start(bf16[1,32,256]{2,1,0:T(8,128)(2,1)S(1)} %get-tuple-element.72), channel_id=1, source_target_pairs={{0,8},{8,16},{16,24},{24,0},{1,9},{9,17},{17,25},{25,1},{2,10},{10... | collective-permute-start | bytes 49160 | tf_op jit(solution)/shard_map/ppermute | solution.py:19
  42.2 52.1 %collective-permute-start.5 = (bf16[4,1,32,256]{3,2,1,0:T(8,128)(2,1)}, bf16[4,1,32,256]{3,2,1,0:T(8,128)(2,1)S(1)}, u32[]{:S(2)}, u32[]{:S(2)}) collective-permute-start(bf16[4,1,32,256]{3,2,1,0:T(8,128)(2,1)} %get-tuple-element.21), channel_id=1, source_target_pairs={{8,0},{16,8},{24,16},{9,1},{17,9},{25,17},{10,2},{18,10},{26,18},{... | collective-permute-start | bytes 196616 | tf_op jit(solution)/shard_map/ppermute | solution.py:21
  83.6 17.3 %collective-permute-start.16 = (bf16[1,32,256]{2,1,0:T(8,128)(2,1)S(1)}, bf16[1,32,256]{2,1,0:T(8,128)(2,1)S(1)}, u32[]{:S(2)}, u32[]{:S(2)}) collective-permute-start(bf16[1,32,256]{2,1,0:T(8,128)(2,1)S(1)} %get-tuple-element.70), channel_id=1, source_target_pairs={{0,8},{8,16},{16,24},{24,0},{1,9},{9,17},{17,25},{25,1},{2,10},{10... | collective-permute-start | bytes 49160 | tf_op jit(solution)/shard_map/ppermute | solution.py:19
  83.7 17.2 %collective-permute-start.17 = (bf16[1,32,256]{2,1,0:T(8,128)(2,1)S(1)}, bf16[1,32,256]{2,1,0:T(8,128)(2,1)S(1)}, u32[]{:S(2)}, u32[]{:S(2)}) collective-permute-start(bf16[1,32,256]{2,1,0:T(8,128)(2,1)S(1)} %get-tuple-element.71), channel_id=1, source_target_pairs={{8,0},{16,8},{24,16},{0,24},{9,1},{17,9},{25,17},{1,25},{10,2},{18... | collective-permute-start | bytes 49160 | tf_op jit(solution)/shard_map/ppermute | solution.py:21
  88.0 32.6 %collective-permute-start.2 = (bf16[4,18,1,256]{3,2,1,0:T(2,128)(2,1)S(1)}, bf16[4,18,1,256]{3,2,1,0:T(2,128)(2,1)S(1)}, u32[]{:S(2)}, u32[]{:S(2)}) collective-permute-start(bf16[4,18,1,256]{3,2,1,0:T(2,128)(2,1)S(1)} %get-tuple-element.20), channel_id=1, source_target_pairs={{0,2},{2,4},{4,6},{1,3},{3,5},{5,7},{8,10},{10,12},{12,14},{9,11},... | collective-permute-start | bytes 110600 | tf_op jit(solution)/shard_map/ppermute | solution.py:19
  92.9 27.6 %collective-permute-start.3 = (bf16[4,18,1,256]{3,2,1,0:T(2,128)(2,1)S(1)}, bf16[4,18,1,256]{3,2,1,0:T(2,128)(2,1)S(1)}, u32[]{:S(2)}, u32[]{:S(2)}) collective-permute-start(bf16[4,18,1,256]{3,2,1,0:T(2,128)(2,1)S(1)} %get-tuple-element.19), channel_id=1, source_target_pairs={{2,0},{4,2},{6,4},{3,1},{5,3},{7,5},{10,8},{12,10},{14,12},{11,9},... | collective-permute-start | bytes 110600 | tf_op jit(solution)/shard_map/ppermute | solution.py:21
  95.1 103.0 %collective-permute-start.6 = (bf16[4,18,1,256]{3,2,1,0:T(2,128)(2,1)}, bf16[4,18,1,256]{3,2,1,0:T(2,128)(2,1)S(1)}, u32[]{:S(2)}, u32[]{:S(2)}) collective-permute-start(bf16[4,18,1,256]{3,2,1,0:T(2,128)(2,1)} %get-tuple-element.15), channel_id=1, source_target_pairs={{2,0},{4,2},{6,4},{3,1},{5,3},{7,5},{10,8},{12,10},{14,12},{11,9},... | collective-permute-start | bytes 110600 | tf_op jit(solution)/shard_map/ppermute | solution.py:21
  107.0 5.6 %collective-permute-start.20 = (bf16[1,32,256]{2,1,0:T(8,128)(2,1)S(1)}, bf16[1,32,256]{2,1,0:T(8,128)(2,1)S(1)}, u32[]{:S(2)}, u32[]{:S(2)}) collective-permute-start(bf16[1,32,256]{2,1,0:T(8,128)(2,1)S(1)} %get-tuple-element.68), channel_id=1, source_target_pairs={{0,8},{8,16},{16,24},{24,0},{1,9},{9,17},{17,25},{25,1},{2,10},{10... | collective-permute-start | bytes 49160 | tf_op jit(solution)/shard_map/ppermute | solution.py:19
  112.6 6.6 %collective-permute-start.23 = (bf16[18,1,256]{2,1,0:T(2,128)(2,1)S(1)}, bf16[18,1,256]{2,1,0:T(2,128)(2,1)S(1)}, u32[]{:S(2)}, u32[]{:S(2)}) collective-permute-start(bf16[18,1,256]{2,1,0:T(2,128)(2,1)S(1)} %get-tuple-element.47), channel_id=1, source_target_pairs={{0,2},{2,4},{4,6},{6,0},{1,3},{3,5},{5,7},{7,1},{8,10},{10,12},{12... | collective-permute-start | bytes 27656 | tf_op jit(solution)/shard_map/ppermute | solution.py:19
  114.7 82.4 %collective-permute-start.7 = (bf16[4,18,1,256]{3,2,1,0:T(2,128)(2,1)}, bf16[4,18,1,256]{3,2,1,0:T(2,128)(2,1)S(1)}, u32[]{:S(2)}, u32[]{:S(2)}) collective-permute-start(bf16[4,18,1,256]{3,2,1,0:T(2,128)(2,1)} %get-tuple-element.14), channel_id=1, source_target_pairs={{0,2},{2,4},{4,6},{1,3},{3,5},{5,7},{8,10},{10,12},{12,14},{9,11},... | collective-permute-start | bytes 110600 | tf_op jit(solution)/shard_map/ppermute | solution.py:19
  163.6 40.4 %collective-permute-start.24 = (bf16[1,32,256]{2,1,0:T(8,128)(2,1)}, bf16[1,32,256]{2,1,0:T(8,128)(2,1)}, u32[]{:S(2)}, u32[]{:S(2)}) collective-permute-start(bf16[1,32,256]{2,1,0:T(8,128)(2,1)} %get-tuple-element.66), channel_id=1, source_target_pairs={{0,8},{8,16},{16,24},{24,0},{1,9},{9,17},{17,25},{25,1},{2,10},{10... | collective-permute-start | bytes 49160 | tf_op jit(solution)/shard_map/ppermute | solution.py:19
  163.6 40.4 %collective-permute-start.25 = (bf16[1,32,256]{2,1,0:T(8,128)(2,1)}, bf16[1,32,256]{2,1,0:T(8,128)(2,1)}, u32[]{:S(2)}, u32[]{:S(2)}) collective-permute-start(bf16[1,32,256]{2,1,0:T(8,128)(2,1)} %get-tuple-element.67), channel_id=1, source_target_pairs={{8,0},{16,8},{24,16},{0,24},{9,1},{17,9},{25,17},{1,25},{10,2},{18... | collective-permute-start | bytes 49160 | tf_op jit(solution)/shard_map/ppermute | solution.py:21
  187.8 145.1 %reduce-scatter.2.cloned.1.call-start = ((), (), s32[]{:S(2)}) async-start(), calls=%async_computation.2 | async-start | bytes 2506752 | tf_op jit(solution)/shard_map/reduce_scatter | solution.py:98
  211.0 5.5 %collective-permute-start.28 = (bf16[1,32,256]{2,1,0:T(8,128)(2,1)S(1)}, bf16[1,32,256]{2,1,0:T(8,128)(2,1)S(1)}, u32[]{:S(2)}, u32[]{:S(2)}) collective-permute-start(bf16[1,32,256]{2,1,0:T(8,128)(2,1)S(1)} %get-tuple-element.64), channel_id=1, source_target_pairs={{0,8},{8,16},{16,24},{24,0},{1,9},{9,17},{17,25},{25,1},{2,10},{10... | collective-permute-start | bytes 49160 | tf_op jit(solution)/shard_map/ppermute | solution.py:19
  254.1 5.5 %collective-permute-start.32 = (bf16[1,32,256]{2,1,0:T(8,128)(2,1)S(1)}, bf16[1,32,256]{2,1,0:T(8,128)(2,1)S(1)}, u32[]{:S(2)}, u32[]{:S(2)}) collective-permute-start(bf16[1,32,256]{2,1,0:T(8,128)(2,1)S(1)} %get-tuple-element.62), channel_id=1, source_target_pairs={{0,8},{8,16},{16,24},{24,0},{1,9},{9,17},{17,25},{25,1},{2,10},{10... | collective-permute-start | bytes 49160 | tf_op jit(solution)/shard_map/ppermute | solution.py:19
  254.1 5.5 %collective-permute-start.33 = (bf16[1,32,256]{2,1,0:T(8,128)(2,1)S(1)}, bf16[1,32,256]{2,1,0:T(8,128)(2,1)S(1)}, u32[]{:S(2)}, u32[]{:S(2)}) collective-permute-start(bf16[1,32,256]{2,1,0:T(8,128)(2,1)S(1)} %get-tuple-element.63), channel_id=1, source_target_pairs={{8,0},{16,8},{24,16},{0,24},{9,1},{17,9},{25,17},{1,25},{10,2},{18... | collective-permute-start | bytes 49160 | tf_op jit(solution)/shard_map/ppermute | solution.py:21
  269.3 5.3 %collective-permute-start.37 = (bf16[1,32,256]{2,1,0:T(8,128)(2,1)S(1)}, bf16[1,32,256]{2,1,0:T(8,128)(2,1)S(1)}, u32[]{:S(2)}, u32[]{:S(2)}) collective-permute-start(bf16[1,32,256]{2,1,0:T(8,128)(2,1)S(1)} %get-tuple-element.61), channel_id=1, source_target_pairs={{8,0},{16,8},{24,16},{0,24},{9,1},{17,9},{25,17},{1,25},{10,2},{18... | collective-permute-start | bytes 49160 | tf_op jit(solution)/shard_map/ppermute | solution.py:21
  273.2 5.5 %collective-permute-start.36 = (bf16[1,32,256]{2,1,0:T(8,128)(2,1)S(1)}, bf16[1,32,256]{2,1,0:T(8,128)(2,1)S(1)}, u32[]{:S(2)}, u32[]{:S(2)}) collective-permute-start(bf16[1,32,256]{2,1,0:T(8,128)(2,1)S(1)} %get-tuple-element.60), channel_id=1, source_target_pairs={{0,8},{8,16},{16,24},{24,0},{1,9},{9,17},{17,25},{25,1},{2,10},{10... | collective-permute-start | bytes 49160 | tf_op jit(solution)/shard_map/ppermute | solution.py:19
  (37 other events, 151.1 us)
Sparse Core Ops, SparseCore 0:
  187.9 40.1 all-reduce.1
  268.1 64.7 reduce-scatter.1
where the time goes:
time: 344 us; the launch traced here: 342 us
  blocking collectives  124 us (36%)
  matrix products  71.3 us (21%)
  starting transfers between devices  56.8 us (17%)
  waiting for transfers between devices  37.9 us (11%)
  between operations  20.3 us (6%)
  other arithmetic  19.6 us (6%)
  local copies, waits for them, and re-layouts  12.2 us (4%)
    psum x3, blocking collectives, per_device(): squared = lax.psum(jnp.sum(back * back), ('rows', 'cols'))  94.5 us
    dot_general x45, matrix products, tap_sum(): jnp.einsum('...c,cd->...d', window, kernel[row_tap, col_tap], preferred_e...  35.2 us
    ppermute x20, starting transfers between devices, extended(): lax.ppermute(head, axis, [((i + 1) % count, i) for i in range(ends)])  31.4 us
    psum x1, blocking collectives, per_device(): lax.psum(jnp.stack([jnp.sum(back * back), jnp.sum(wide_iter * wide_iter)]...  29.9 us
    ppermute x20, starting transfers between devices, extended(): lax.ppermute(tail, axis, [(i, (i + 1) % count) for i in range(ends)])  25.1 us
    dot_general x45, matrix products, tap_sum(): jnp.einsum('...d,cd->...c', window, kernel[row_tap, col_tap], preferred_e...  24.5 us
    ppermute x20, waiting for transfers between devices, extended(): lax.ppermute(tail, axis, [(i, (i + 1) % count) for i in range(ends)])  17.7 us
    reduce_scatter x1, waiting for transfers between devices, per_device(): lax.psum_scatter(replica_total, ('rows', 'cols'), scatter_dimension=0, ti...  12.6 us
  transfers between devices with their start and end apart: 42, of which 20 were waited for; matrix products, arithmetic and copies ran while one was open for 27% of the time, Pallas kernels for 0%

commit v1 on v0

v1 whole, which is shorter than its diff:
```python
import functools
import math

import jax
import jax.numpy as jnp
from jax import lax
from jax.experimental import pallas as pl
from jax.experimental.pallas import tpu as pltpu
from jax.sharding import PartitionSpec as P

MESH = pl.DeviceIdType.MESH
ITERS = 4
F32 = jnp.float32
BF16 = jnp.bfloat16
SIDES = [(v, h) for v in (-1, 0, 1) for h in (-1, 0, 1) if (v, h) != (0, 0)]


def split_rows(rows):
    for block in (13, 11, 10, 9, 8, 7, 6, 5, 4, 3, 2):
        if rows % block == 0:
            return block
    return 1


def kernel(
    nr, nc, counts, in_ref, up_ref, k_ref, p_ref,
    o_ref, g_ref, kg_ref, po_ref, sc_ref,
    fs_row, fr_row, fs_col, fr_col, fs_cor, fr_cor,
    pb, pr_row, ps_col, pr_col, ps_cor, pr_cor,
    xin, xup, xa, xb, wt, ut, gb, r0, h1, r1, h2, r2, h3, r3, tab,
    f_send, f_recv, p_send, p_recv, s0, s1s, s1r, s2s, s2r, s3, ts, tr,
):
    batch, height, breadth, ch = in_ref.shape
    halo = 2 * ITERS
    wide = breadth + 2 * halo
    cell_count, grad_scale = counts
    n = nr * nc
    half = nc // 2
    ri, ci, rp = lax.axis_index("rows"), lax.axis_index("cols"), lax.axis_index("rep")
    me = ri * nc + ci
    core, cy = lax.rem(ci, 2), ci // 2

    def dev(row, col, rep):
        return {"rows": row, "cols": col, "rep": rep}

    barrier = pltpu.get_barrier_semaphore()

    def greet(k, c):
        t = lax.rem(me + k, n)
        pl.semaphore_signal(
            barrier, inc=1, device_id=dev(t // nc, lax.rem(t, nc), rp), device_id_type=MESH
        )
        return c

    lax.fori_loop(1, n, greet, 0)
    pl.semaphore_signal(barrier, inc=1, device_id=dev(ri, ci, 1 - rp), device_id_type=MESH)

    for f, ref in ((0, in_ref), (1, up_ref)):
        lo = f * batch
        for s, row in ((0, 0), (1, height - 1)):
            fs_row[s, lo : lo + batch] = ref[:, row]
        for b in range(batch):
            x = ref[b].astype(F32)
            left, right = x[:, 0, :], x[:, breadth - 1, :]
            fs_col[0, lo + b] = left.astype(BF16)
            fs_col[1, lo + b] = right.astype(BF16)
            for h, edge in ((0, left), (1, right)):
                fs_cor[0, h, lo + b] = jnp.broadcast_to(edge[0:1], (16, ch)).astype(BF16)
                fs_cor[1, h, lo + b] = jnp.broadcast_to(
                    edge[height - 1 : height], (16, ch)
                ).astype(BF16)
    pb[...] = p_ref[...].astype(BF16)
    for h, col in ((0, 0), (1, breadth - halo)):
        edge = p_ref[:, col : col + halo, :]
        ps_col[h] = edge.reshape(height * halo // 16, 16, ch).astype(BF16)
        for v, row in ((0, 0), (1, height - halo)):
            ps_cor[v, h] = (
                edge[row : row + halo].reshape(halo * halo // 16, 16, ch).astype(BF16)
            )

    pl.semaphore_wait(barrier, n)

    def sidx(v):
        return 0 if v < 0 else 1

    def exists(v, h):
        ok = None
        for d, pos, size in ((v, ri, nr), (h, ci, nc)):
            if d:
                here = (pos > 0) if d < 0 else (pos < size - 1)
                ok = here if ok is None else jnp.logical_and(ok, here)
        return ok

    def target(v, h):
        return dev(lax.rem(ri + v + nr, nr), lax.rem(ci + h + nc, nc), rp)

    def buffers(v, h, row, col, cor):
        if h == 0:
            return row.at[sidx(v)]
        if v == 0:
            return col.at[sidx(h)]
        return cor.at[sidx(v), sidx(h)]

    def f_copy(k):
        v, h = SIDES[k]
        return pltpu.make_async_remote_copy(
            src_ref=buffers(v, h, fs_row, fs_col, fs_cor),
            dst_ref=buffers(-v, -h, fr_row, fr_col, fr_cor),
            send_sem=f_send.at[k],
            recv_sem=f_recv.at[k],
            device_id=target(v, h),
            device_id_type=MESH,
        )

    def p_copy(k):
        v, h = SIDES[k]
        if h == 0:
            src = pb.at[pl.ds(0 if v < 0 else height - halo, halo)]
        else:
            src = buffers(v, h, None, ps_col, ps_cor)
        return pltpu.make_async_remote_copy(
            src_ref=src,
            dst_ref=buffers(-v, -h, pr_row, pr_col, pr_cor),
            send_sem=p_send.at[k],
            recv_sem=p_recv.at[k],
            device_id=target(v, h),
            device_id_type=MESH,
        )

    for k, (v, h) in enumerate(SIDES):
        @pl.when(exists(v, h))
        def _(k=k):
            f_copy(k).start()

        @pl.when(jnp.logical_not(exists(v, h)))
        def _(v=v, h=h):
            ref = buffers(v, h, fr_row, fr_col, fr_cor)
            ref[...] = jnp.zeros(ref.shape, BF16)

    for k in range(8):
        p_copy(k).start()

    for a in range(3):
        for b in range(3):
            wt[a, b * ch : (b + 1) * ch, :] = k_ref[2 - a, 2 - b].T
    cells = height * breadth

    def turn(b, c):
        ut[b] = up_ref[b].reshape(cells, ch).T
        return c

    lax.fori_loop(0, batch, turn, 0)

    for k, (v, h) in enumerate(SIDES):
        @pl.when(exists(-v, -h))
        def _(k=k):
            f_copy(k).wait_recv()

    def put_padded(dst, b, row, value, lefts, rights):
        rows = value.shape[0]
        flat = value.reshape(rows * breadth, ch)
        j = lax.broadcasted_iota(jnp.int32, (rows, breadth, ch), 1)
        left = pltpu.roll(flat, 1, 0).reshape(rows, breadth, ch)
        right = pltpu.roll(flat, rows * breadth - 1, 0).reshape(rows, breadth, ch)
        left = jnp.where(j == 0, lefts[:, None, :], left)
        right = jnp.where(j == breadth - 1, rights[:, None, :], right)
        dst[b, row : row + rows, :, 0:ch] = left.astype(BF16)
        dst[b, row : row + rows, :, ch : 2 * ch] = value.astype(BF16)
        dst[b, row : row + rows, :, 2 * ch :] = right.astype(BF16)

    def pad_fields(f, ref, dst):
        def step(b, c):
            e = f * batch + b
            put_padded(
                dst, b, 1, ref[b].astype(F32),
                fr_col[0, e].astype(F32), fr_col[1, e].astype(F32),
            )
            for s, row in ((0, 0), (1, height + 1)):
                put_padded(
                    dst, b, row, fr_row[s, e].astype(F32)[None],
                    fr_cor[s, 0, e].astype(F32)[0:1], fr_cor[s, 1, e].astype(F32)[0:1],
                )
            return c

        lax.fori_loop(0, batch, step, 0)

    pad_fields(0, in_ref, xin)

    dper = ch // n

    def grad_step(a, c):
        for b in range(3):
            acc = None
            for m in range(batch):
                window = xin[m, pl.ds(a, height), :, b * ch : (b + 1) * ch]
                term = jnp.dot(
                    ut[m], window.reshape(cells, ch), preferred_element_type=F32
                )
                acc = term if acc is None else acc + term
            at = pl.multiple_of(a * (3 * ch) + b * ch, 128)
            for t in range(n):
                rr, cc = t // nc, t % nc
                gb[cc % 2, cc // 2, rr, :, pl.ds(at, ch)] = acc[
                    t * dper : (t + 1) * dper
                ].astype(BF16)
        return c

    lax.fori_loop(0, 3, grad_step, 0)

    def copy0():
        return pltpu.make_async_remote_copy(
            src_ref=gb.at[1 - core],
            dst_ref=r0,
            send_sem=s0.at[0],
            recv_sem=s0.at[1],
            device_id=dev(ri, ci + 1 - 2 * core, rp),
            device_id_type=MESH,
        )

    def copy1(k):
        to = lax.rem(cy + k, half)
        return pltpu.make_async_remote_copy(
            src_ref=h1.at[to],
            dst_ref=r1.at[k - 1],
            send_sem=s1s.at[k - 1],
            recv_sem=s1r.at[k - 1],
            device_id=dev(ri, to * 2 + core, rp),
            device_id_type=MESH,
        )

    def copy2(k):
        to = lax.rem(ri + k, nr)
        return pltpu.make_async_remote_copy(
            src_ref=h2.at[to],
            dst_ref=r2.at[k - 1],
            send_sem=s2s.at[k - 1],
            recv_sem=s2r.at[k - 1],
            device_id=dev(to, ci, rp),
            device_id_type=MESH,
        )

    def copy3():
        return pltpu.make_async_remote_copy(
            src_ref=h3,
            dst_ref=r3,
            send_sem=s3.at[0],
            recv_sem=s3.at[1],
            device_id=dev(ri, ci, 1 - rp),
            device_id_type=MESH,
        )

    copy0().start()

    def field_conv(src, dst, weights):
        block = min(height, 8)

        def step(t, c):
            b, row = t // (height // block), lax.rem(t, height // block) * block
            acc = None
            for a in range(3):
                window = src[b, pl.ds(row + a, block)].reshape(block * breadth, 3 * ch)
                term = jnp.dot(window, weights(a), preferred_element_type=F32)
                acc = term if acc is None else acc + term
            dst[b, pl.ds(row, block)] = acc.reshape(block, breadth, ch).astype(BF16)
            return c

        lax.fori_loop(0, batch * (height // block), step, 0)

    def forward(a):
        return k_ref[a].reshape(3 * ch, ch)

    def adjoint(a):
        return wt[a]

    field_conv(xin, o_ref, forward)

    copy0().wait_recv()

    def sum0(t, c):
        a, b = t // nr, lax.rem(t, nr)
        h1[a, b] = (gb[core, a, b].astype(F32) + r0[a, b].astype(F32)).astype(BF16)
        return c

    lax.fori_loop(0, half * nr, sum0, 0)
    for k in range(1, half):
        copy1(k).start()

    pad_fields(1, up_ref, xup)

    def put(dst, row, value):
        rows = value.shape[0]
        flat = value.reshape(rows * wide, ch)
        left = pltpu.roll(flat, 1, 0)
        right = pltpu.roll(flat, rows * wide - 1, 0)
        dst[pl.ds(row, rows), :, 0:ch] = left.reshape(rows, wide, ch).astype(BF16)
        dst[pl.ds(row, rows), :, ch : 2 * ch] = value.astype(BF16)
        dst[pl.ds(row, rows), :, 2 * ch :] = right.reshape(rows, wide, ch).astype(BF16)

    for k in range(8):
        p_copy(k).wait_recv()
    for s, row in ((0, 0), (1, height + halo)):
        put(
            xa, row,
            jnp.concatenate(
                [
                    pr_cor[s, 0].astype(F32).reshape(halo, halo, ch),
                    pr_row[s].astype(F32),
                    pr_cor[s, 1].astype(F32).reshape(halo, halo, ch),
                ],
                axis=1,
            ),
        )
    put(
        xa, halo,
        jnp.concatenate(
            [
                pr_col[0].astype(F32).reshape(height, halo, ch),
                pb[...].astype(F32),
                pr_col[1].astype(F32).reshape(height, halo, ch),
            ],
            axis=1,
        ),
    )

    def tile_conv(src, row, block, weights):
        acc = None
        for a in range(3):
            window = src[pl.ds(row + a, block)].reshape(block * wide, 3 * ch)
            term = jnp.dot(window, weights(a), preferred_element_type=F32)
            acc = term if acc is None else acc + term
        return acc

    def fold(x):
        return jnp.sum(x.reshape(-1, 8, ch), axis=0)

    def total(x):
        return jnp.sum(jnp.sum(x, axis=0, keepdims=True), axis=1, keepdims=True)

    def note(row, value):
        tab[me, row : row + 1, :] = jnp.broadcast_to(value, (1, 128))

    factor = None
    rows = height + 2 * halo
    for it in range(ITERS):
        rows -= 2
        block = split_rows(rows)

        def ahead(t, c, block=block, factor=factor):
            acc = tile_conv(xa, t * block, block, forward)
            if factor is not None:
                acc = acc * factor
            put(xb, t * block, acc.reshape(block, wide, ch))
            return c

        lax.fori_loop(0, rows // block, ahead, 0)
        rows -= 2
        block = split_rows(rows)
        first = (rows - height) // 2
        last = it + 1 == ITERS

        def back(t, c, block=block, first=first, last=last):
            own, every, rounded = c
            acc = tile_conv(xb, t * block, block, adjoint)
            full = acc.reshape(block, wide, ch)
            mine = full[:, halo : halo + breadth, :]
            if last:
                po_ref[pl.ds(t * block, block)] = mine
                return own + fold(mine * mine), every, rounded
            put(xa, t * block, full)
            where = t * block + lax.broadcasted_iota(jnp.int32, mine.shape, 0)
            inside = jnp.logical_and(where >= first, where < first + height)
            mine = jnp.where(inside, mine, 0.0)
            near = mine.astype(BF16).astype(F32)
            return (
                own + fold(mine * mine),
                every + fold(acc * acc),
                rounded + fold(near * near),
            )

        zero = jnp.zeros((8, ch), F32)
        own, every, rounded = lax.fori_loop(0, rows // block, back, (zero, zero, zero))
        note(it, total(own))
        if it == ITERS - 2:
            note(ITERS, total(rounded))
        if not last:
            mean = total(every) / float(rows * wide * ch)
            root = jnp.sqrt(jnp.maximum(mean, 1e-30))
            factor = 1.0 / root
            note(ITERS + 1 + it, root)
        if it == 0:
            for k in range(1, half):
                copy1(k).wait_recv()

            def sum1(b, c):
                acc = h1[cy, b].astype(F32)
                for k in range(1, half):
                    acc = acc + r1[k - 1, b].astype(F32)
                h2[b] = acc.astype(BF16)
                return c

            lax.fori_loop(0, nr, sum1, 0)
            for k in range(1, nr):
                copy2(k).start()
        if it == ITERS - 2:
            for k in range(1, nr):
                copy2(k).wait_recv()
            acc = h2[ri].astype(F32)
            for k in range(1, nr):
                acc = acc + r2[k - 1].astype(F32)
            h3[...] = acc
            copy3().start()

    def copyt(k):
        to = lax.rem(me + k, n)
        return pltpu.make_async_remote_copy(
            src_ref=tab.at[me],
            dst_ref=tab.at[me],
            send_sem=ts.at[k],
            recv_sem=tr.at[k],
            device_id=dev(to // nc, lax.rem(to, nc), rp),
            device_id_type=MESH,
        )

    def copyt_in(k):
        of = lax.rem(me - k + n, n)
        return pltpu.make_async_remote_copy(
            src_ref=tab.at[me],
            dst_ref=tab.at[of],
            send_sem=ts.at[k],
            recv_sem=tr.at[k],
            device_id=dev(of // nc, lax.rem(of, nc), rp),
            device_id_type=MESH,
        )

    def tell(k, c):
        copyt(k).start()
        return c

    lax.fori_loop(1, n, tell, 0)

    field_conv(xup, g_ref, adjoint)

    def hear(k, c):
        copyt_in(k).wait_recv()
        return c

    lax.fori_loop(1, n, hear, 0)
    told = tab[...]
    gain = jnp.ones((n, 128), F32)
    for it in range(ITERS - 1):
        squared = jnp.sum(told[:, it, :] * gain * gain, axis=0, keepdims=True)
        scale = jnp.sqrt(squared / cell_count + 1e-06)
        sc_ref[it + 1 : it + 2, :] = scale
        gain = gain / scale
        if it == ITERS - 2:
            sum_probe = jnp.sum(told[:, ITERS, :] * gain * gain, axis=0, keepdims=True)
        gain = gain * told[:, ITERS + 1 + it, :]
    sum_back = jnp.sum(told[:, ITERS - 1, :] * gain * gain, axis=0, keepdims=True)
    sc_ref[0:1, :] = jnp.sqrt(jnp.sqrt(sum_back / sum_probe))
    own_gain = 1.0 / jnp.sqrt(sum_back / cell_count + 1e-06)
    for it in range(ITERS - 1):
        own_gain = own_gain * tab[me, ITERS + 1 + it : ITERS + 2 + it, :]
        own_gain = own_gain / sc_ref[it + 1 : it + 2, :]
    both = jnp.concatenate([own_gain] * (ch // 128), axis=1).reshape(1, 1, ch)
    po_ref[...] = po_ref[...] * both

    copy3().wait_recv()
    kg_ref[...] = (h3[...] + r3[...]) * grad_scale

    for k, (v, h) in enumerate(SIDES):
        @pl.when(exists(v, h))
        def _(k=k):
            f_copy(k).wait_send()

        p_copy(k).wait_send()
    copy0().wait_send()
    for k in range(1, half):
        copy1(k).wait_send()
    for k in range(1, nr):
        copy2(k).wait_send()
    copy3().wait_send()

    def sent(k, c):
        copyt(k).wait_send()
        return c

    lax.fori_loop(1, n, sent, 0)


def solution(mesh):
    nr, nc = mesh.shape["rows"], mesh.shape["cols"]
    reps = mesh.shape["rep"]

    def per_device(inputs, upstream, weights, probe_init):
        batch, height, breadth, ch = inputs.shape
        n = nr * nc
        half = nc // 2
        dper = ch // n
        halo = 2 * ITERS
        wide = breadth + 2 * halo
        cell_count = float(height * nr * breadth * nc * ch)
        grad_scale = 1.0 / math.sqrt(batch * reps * height * nr * breadth * nc)
        cells = height * breadth
        sem = pltpu.SemaphoreType.DMA
        vmem = pl.BlockSpec(memory_space=pltpu.VMEM)
        scratch = [
            ((2, 2 * batch, breadth, ch), BF16),
            ((2, 2 * batch, breadth, ch), BF16),
            ((2, 2 * batch, height, ch), BF16),
            ((2, 2 * batch, height, ch), BF16),
            ((2, 2, 2 * batch, 16, ch), BF16),
            ((2, 2, 2 * batch, 16, ch), BF16),
            ((height, breadth, ch), BF16),
            ((2, halo, breadth, ch), BF16),
            ((2, height * halo // 16, 16, ch), BF16),
            ((2, height * halo // 16, 16, ch), BF16),
            ((2, 2, halo * halo // 16, 16, ch), BF16),
            ((2, 2, halo * halo // 16, 16, ch), BF16),
            ((batch, height + 2, breadth, 3 * ch), BF16),
            ((batch, height + 2, breadth, 3 * ch), BF16),
            ((height + 2 * halo, wide, 3 * ch), BF16),
            ((height + 2 * halo, wide, 3 * ch), BF16),
            ((3, 3 * ch, ch), BF16),
            ((batch, ch, cells), BF16),
            ((2, half, nr, dper, 9 * ch), BF16),
            ((half, nr, dper, 9 * ch), BF16),
            ((half, nr, dper, 9 * ch), BF16),
            ((half - 1, nr, dper, 9 * ch), BF16),
            ((nr, dper, 9 * ch), BF16),
            ((nr - 1, dper, 9 * ch), BF16),
            ((dper, 9 * ch), F32),
            ((dper, 9 * ch), F32),
            ((n, 8, 128), F32),
        ]
        outs = pl.pallas_call(
            functools.partial(kernel, nr, nc, (cell_count, grad_scale)),
            out_shape=(
                jax.ShapeDtypeStruct(inputs.shape, BF16),
                jax.ShapeDtypeStruct(inputs.shape, BF16),
                jax.ShapeDtypeStruct((dper, 9 * ch), F32),
                jax.ShapeDtypeStruct(probe_init.shape, F32),
                jax.ShapeDtypeStruct((8, 128), F32),
            ),
            in_specs=[vmem] * 4,
            out_specs=[vmem] * 5,
            scratch_shapes=[pltpu.VMEM(s, t) for s, t in scratch]
            + [
                sem((8,)), sem((8,)), sem((8,)), sem((8,)), sem((2,)),
                sem((max(half - 1, 1),)), sem((max(half - 1, 1),)),
                sem((nr - 1,)), sem((nr - 1,)), sem((2,)), sem((n,)), sem((n,)),
            ],
            compiler_params=pltpu.CompilerParams(
                collective_id=0, has_side_effects=True, vmem_limit_bytes=60 * 2**20
            ),
        )(inputs, upstream, weights, probe_init)
        outputs, input_grad, kernel_grad, probe_out, scalars = outs
        return (
            outputs, input_grad, kernel_grad, probe_out,
            scalars[0, 0], scalars[1:ITERS, 0],
        )

    placed = (
        P("rep", "rows", "cols", None),
        P("rep", "rows", "cols", None),
        P(),
        P("rows", "cols", None),
    )
    return jax.shard_map(
        per_device,
        mesh=mesh,
        in_specs=placed,
        out_specs=(
            P("rep", "rows", "cols", None),
            P("rep", "rows", "cols", None),
            P(("rows", "cols"), None),
            P("rows", "cols", None),
            P(),
            P(),
        ),
        check_vma=False,
    )
```

time: 344 us -> 57.3 us (0.17)
  blocking collectives: 124 us -> 0 us
  matrix products: 71.3 us -> 0 us
  starting transfers between devices: 56.8 us -> 0 us
  Pallas kernels: 0 us -> 49.1 us
  waiting for transfers between devices: 37.9 us -> 0 us
  between operations: 20.3 us -> 0.65 us
  other arithmetic: 19.6 us -> 0 us
  local copies, waits for them, and re-layouts: 12.2 us -> 7.32 us
    psum x4 -> x0, blocking collectives: 124 us -> none  [the longest x3 94.5 us: per_device(): squared = lax.psum(jnp.sum(back * back), ('rows', 'cols'))]
    dot_general x99 -> x0, matrix products: 71.3 us -> none  [the longest x45 35.2 us: tap_sum(): jnp.einsum('...c,cd->...d', window, kernel[row_tap, col_tap], preferred_e...]
    ppermute x40 -> x0, starting transfers between devices: 56.5 us -> none  [the longest x20 31.4 us: extended(): lax.ppermute(head, axis, [((i + 1) % count, i) for i in range(ends)])]
    pallas_call x0 -> x1, Pallas kernels: none -> 49.1 us  [per_device(): pl.pallas_call(functools.partial(kernel, nr, nc, (cell_count, grad_scale)...]
    ppermute x40 -> x0, waiting for transfers between devices: 25.2 us -> none  [the longest x20 17.7 us: extended(): lax.ppermute(tail, axis, [(i, (i + 1) % count) for i in range(ends)])]
    reduce_scatter x1 -> x0, waiting for transfers between devices: 12.6 us -> none  [per_device(): lax.psum_scatter(replica_total, ('rows', 'cols'), scatter_dimension=0, ti...]
    concatenate x9 -> x0, other arithmetic: 7.32 us -> none  [extended(): jnp.concatenate([lax.ppermute(tail, axis, [(i, (i + 1) % count) for i in...]
    convert_element_type x4 -> x0, other arithmetic: 6.16 us -> none  [the longest x1 2.83 us: per_device(): lax.psum(local_grad.astype(jnp.bfloat16), 'rep').astype(jnp.float32)]
  transfers between devices with their start and end apart: 42 -> 0, of which waited for: 20 -> 0; matrix products, arithmetic and copies ran while one was open for 27% -> 0% of each run, Pallas kernels for 0% -> 0%
where the time goes in v1:
time: 57.3 us; the launch traced here: 57.1 us
  Pallas kernels  49.1 us (86%)
  local copies, waits for them, and re-layouts  7.32 us (13%)
  between operations  0.65 us (1%)
    pallas_call x1, Pallas kernels, per_device(): pl.pallas_call(functools.partial(kernel, nr, nc, (cell_count, grad_scale)...  49.1 us
    unnamed x10, local copies, waits for them, and re-layouts  4.75 us
    slice x1, local copies, waits for them, and re-layouts, per_device(): scalars[1:ITERS, 0]  1.3 us
    slice x1, local copies, waits for them, and re-layouts, per_device(): scalars[0, 0]  1.27 us

profile of v1, /device:TPU:0, one launch (start us, length us, event | category | flops | bytes accessed | tf_op | source)
XLA Modules:
  0.0 57.1 jit_solution(8183048988167577874)
XLA Ops:
  0.6 49.1 %shard_map.91 = (bf16[4,16,32,256]{3,2,1,0:T(8,128)(2,1)}, bf16[4,16,32,256]{3,2,1,0:T(8,128)(2,1)}, f32[16,2304]{1,0:T(8,128)}, f32[16,32,256]{2,1,0:T(8,128)}, f32[8,128]{1,0:T(8,128)}) custom-call(bf16[4,16,32,256]{3,2,1,0:T(8,128)(2,1)} %in_ref.1, bf16[4,16,32,256]{3,2,1,0:T(8,128)(2,1)} %up_ref.1, bf16[3,3,256,256]{3,2,1,0:T(8,128)(2,1)} %k_ref.1, ...), custom_call_target="tpu_custom_call" | custom-call | tf_op jit(solution)/shard_map/pallas_call | solution.py:535
  49.7 0.0 copy-start
  49.7 1.3 %slice.6 = f32[1,1]{1,0:T(1,128)} slice(f32[8,128]{1,0:T(8,128)} %get-tuple-element.15), slice={[0:1], [0:1]} | slice | bytes 8 | tf_op jit(solution)/shard_map/slice | solution.py:559
  51.0 1.3 %slice_reduce_fusion = f32[3]{0:T(128)} fusion(f32[8,128]{1,0:T(8,128)} %get-tuple-element.15), kind=kLoop, calls=%fused_computation | loop fusion | bytes 24 | tf_op jit(solution)/shard_map/slice | solution.py:559
  52.3 2.3 %copy.14 = bf16[4,16,32,256]{3,2,1,0:T(8,128)(2,1)} copy(bf16[4,16,32,256]{3,2,1,0:T(8,128)(2,1)} %get-tuple-element.22) | data formatting | bytes 2097152
  54.6 0.0 copy-done
  54.6 0.0 copy-start.2
  54.6 0.0 copy-start.1
  54.6 1.0 %copy.15 = bf16[4,16,32,256]{3,2,1,0:T(8,128)(2,1)} copy(bf16[4,16,32,256]{3,2,1,0:T(8,128)(2,1)S(1)} %copy-done) | data formatting | bytes 2097152
  55.5 0.1 copy-done.2
  55.6 0.7 %copy.16 = f32[16,2304]{1,0:T(8,128)} copy(f32[16,2304]{1,0:T(8,128)S(1)} %copy-done.2) | data formatting | bytes 294912
  56.3 0.0 copy-done.1
  56.3 0.8 %copy.17 = f32[16,32,256]{2,1,0:T(8,128)} copy(f32[16,32,256]{2,1,0:T(8,128)S(1)} %copy-done.1) | data formatting | bytes 1048576
Async XLA Ops:
  49.7 4.8 %copy-start = (bf16[4,16,32,256]{3,2,1,0:T(8,128)(2,1)S(1)}, bf16[4,16,32,256]{3,2,1,0:T(8,128)(2,1)}, u32[]{:S(2)}) copy-start(bf16[4,16,32,256]{3,2,1,0:T(8,128)(2,1)} %get-tuple-element.23) | copy-start | bytes 3145732
  54.6 1.0 %copy-start.2 = (f32[16,2304]{1,0:T(8,128)S(1)}, f32[16,2304]{1,0:T(8,128)}, u32[]{:S(2)}) copy-start(f32[16,2304]{1,0:T(8,128)} %get-tuple-element.24) | copy-start | bytes 442372
  54.6 1.7 %copy-start.1 = (f32[16,32,256]{2,1,0:T(8,128)S(1)}, f32[16,32,256]{2,1,0:T(8,128)}, u32[]{:S(2)}) copy-start(f32[16,32,256]{2,1,0:T(8,128)} %get-tuple-element.25) | copy-start | bytes 1572868

commit v2 on v1

--- a/solution.py
+++ b/solution.py
@@ -23,8 +23,9 @@
 
 
 def kernel(
-    nr, nc, counts, in_ref, up_ref, k_ref, p_ref,
-    o_ref, g_ref, kg_ref, po_ref, sc_ref,
+    nr, nc, counts, in_hbm, up_hbm, k_hbm, p_hbm,
+    o_hbm, g_hbm, kg_ref, po_ref, sc_ref,
+    in_ref, up_ref, k_ref, p_ref, o_ref, g_ref, load, store,
     fs_row, fr_row, fs_col, fr_col, fs_cor, fr_cor,
     pb, pr_row, ps_col, pr_col, ps_cor, pr_cor,
     xin, xup, xa, xb, wt, ut, gb, r0, h1, r1, h2, r2, h3, r3, tab,
@@ -34,6 +35,18 @@
     halo = 2 * ITERS
     wide = breadth + 2 * halo
     cell_count, grad_scale = counts
+    loads = [
+        pltpu.make_async_copy(src, dst, load.at[i])
+        for i, (src, dst) in enumerate(
+            ((in_hbm, in_ref), (up_hbm, up_ref), (p_hbm, p_ref), (k_hbm, k_ref))
+        )
+    ]
+    stores = [
+        pltpu.make_async_copy(src, dst, store.at[i])
+        for i, (src, dst) in enumerate(((o_ref, o_hbm), (g_ref, g_hbm)))
+    ]
+    for one in loads:
+        one.start()
     n = nr * nc
     half = nc // 2
     ri, ci, rp = lax.axis_index("rows"), lax.axis_index("cols"), lax.axis_index("rep")
@@ -57,6 +70,7 @@
 
     for f, ref in ((0, in_ref), (1, up_ref)):
         lo = f * batch
+        loads[f].wait()
         for s, row in ((0, 0), (1, height - 1)):
             fs_row[s, lo : lo + batch] = ref[:, row]
         for b in range(batch):
@@ -69,6 +83,7 @@
                 fs_cor[1, h, lo + b] = jnp.broadcast_to(
                     edge[height - 1 : height], (16, ch)
                 ).astype(BF16)
+    loads[2].wait()
     pb[...] = p_ref[...].astype(BF16)
     for h, col in ((0, 0), (1, breadth - halo)):
         edge = p_ref[:, col : col + halo, :]
@@ -140,13 +155,17 @@
     for k in range(8):
         p_copy(k).start()
 
+    loads[3].wait()
+
     for a in range(3):
         for b in range(3):
             wt[a, b * ch : (b + 1) * ch, :] = k_ref[2 - a, 2 - b].T
     cells = height * breadth
 
     def turn(b, c):
-        ut[b] = up_ref[b].reshape(cells, ch).T
+        ut[:, pl.ds(pl.multiple_of(b * cells, 128), cells)] = (
+            up_ref[b].reshape(cells, ch).T
+        )
         return c
 
     lax.fori_loop(0, batch, turn, 0)
@@ -190,13 +209,10 @@
 
     def grad_step(a, c):
         for b in range(3):
-            acc = None
-            for m in range(batch):
-                window = xin[m, pl.ds(a, height), :, b * ch : (b + 1) * ch]
-                term = jnp.dot(
-                    ut[m], window.reshape(cells, ch), preferred_element_type=F32
-                )
-                acc = term if acc is None else acc + term
+            window = xin[:, pl.ds(a, height), :, b * ch : (b + 1) * ch]
+            acc = jnp.dot(
+                ut[...], window.reshape(batch * cells, ch), preferred_element_type=F32
+            )
             at = pl.multiple_of(a * (3 * ch) + b * ch, 128)
             for t in range(n):
                 rr, cc = t // nc, t % nc
@@ -256,23 +272,26 @@
 
         def step(t, c):
             b, row = t // (height // block), lax.rem(t, height // block) * block
-            acc = None
-            for a in range(3):
-                window = src[b, pl.ds(row + a, block)].reshape(block * breadth, 3 * ch)
-                term = jnp.dot(window, weights(a), preferred_element_type=F32)
-                acc = term if acc is None else acc + term
+            windows = [
+                src[b, pl.ds(row + a, block)].reshape(block * breadth, 3 * ch)
+                for a in range(3)
+            ]
+            acc = jnp.dot(
+                jnp.concatenate(windows, axis=1), weights(), preferred_element_type=F32
+            )
             dst[b, pl.ds(row, block)] = acc.reshape(block, breadth, ch).astype(BF16)
             return c
 
         lax.fori_loop(0, batch * (height // block), step, 0)
 
-    def forward(a):
-        return k_ref[a].reshape(3 * ch, ch)
-
-    def adjoint(a):
-        return wt[a]
+    def forward():
+        return k_ref[...].reshape(9 * ch, ch)
+
+    def adjoint():
+        return wt[...].reshape(9 * ch, ch)
 
     field_conv(xin, o_ref, forward)
+    stores[0].start()
 
     copy0().wait_recv()
 
@@ -323,12 +342,12 @@
     )
 
     def tile_conv(src, row, block, weights):
-        acc = None
-        for a in range(3):
-            window = src[pl.ds(row + a, block)].reshape(block * wide, 3 * ch)
-            term = jnp.dot(window, weights(a), preferred_element_type=F32)
-            acc = term if acc is None else acc + term
-        return acc
+        windows = [
+            src[pl.ds(row + a, block)].reshape(block * wide, 3 * ch) for a in range(3)
+        ]
+        return jnp.dot(
+            jnp.concatenate(windows, axis=1), weights(), preferred_element_type=F32
+        )
 
     def fold(x):
         return jnp.sum(x.reshape(-1, 8, ch), axis=0)
@@ -439,6 +458,7 @@
     lax.fori_loop(1, n, tell, 0)
 
     field_conv(xup, g_ref, adjoint)
+    stores[1].start()
 
     def hear(k, c):
         copyt_in(k).wait_recv()
@@ -480,11 +500,33 @@
         copy2(k).wait_send()
     copy3().wait_send()
 
+    for one in stores:
+        one.wait()
+
     def sent(k, c):
         copyt(k).wait_send()
         return c
 
     lax.fori_loop(1, n, sent, 0)
+
+
+def finish(o_in, g_in, kg_in, po_in, sc_in, o_out, g_out, kg_out, po_out, lip, trace, sems):
+    copies = []
+    for a in range(o_in.shape[0]):
+        copies.append((o_in.at[a], o_out.at[a]))
+        copies.append((g_in.at[a], g_out.at[a]))
+    copies.append((po_in, po_out))
+    copies.append((kg_in, kg_out))
+    started = [
+        pltpu.make_async_copy(src, dst, sems.at[i]) for i, (src, dst) in enumerate(copies)
+    ]
+    for one in started:
+        one.start()
+    lip[0] = sc_in[0, 0]
+    for i in range(ITERS - 1):
+        trace[i] = sc_in[i + 1, 0]
+    for one in started:
+        one.wait()
 
 
 def solution(mesh):
@@ -521,7 +563,7 @@
             ((height + 2 * halo, wide, 3 * ch), BF16),
             ((height + 2 * halo, wide, 3 * ch), BF16),
             ((3, 3 * ch, ch), BF16),
-            ((batch, ch, cells), BF16),
+            ((ch, batch * cells), BF16),
             ((2, half, nr, dper, 9 * ch), BF16),
             ((half, nr, dper, 9 * ch), BF16),
             ((half, nr, dper, 9 * ch), BF16),
@@ -532,6 +574,11 @@
             ((dper, 9 * ch), F32),
             ((n, 8, 128), F32),
         ]
+        anywhere = pl.BlockSpec(memory_space=pl.ANY)
+        staged = [
+            (inputs.shape, BF16), (inputs.shape, BF16), (weights.shape, BF16),
+            (probe_init.shape, F32), (inputs.shape, BF16), (inputs.shape, BF16),
+        ]
         outs = pl.pallas_call(
             functools.partial(kernel, nr, nc, (cell_count, grad_scale)),
             out_shape=(
@@ -541,9 +588,11 @@
                 jax.ShapeDtypeStruct(probe_init.shape, F32),
                 jax.ShapeDtypeStruct((8, 128), F32),
             ),
-            in_specs=[vmem] * 4,
-            out_specs=[vmem] * 5,
-            scratch_shapes=[pltpu.VMEM(s, t) for s, t in scratch]
+            in_specs=[anywhere] * 4,
+            out_specs=[anywhere] * 2 + [vmem] * 3,
+            scratch_shapes=[pltpu.VMEM(s, t) for s, t in staged]
+            + [sem((4,)), sem((2,))]
+            + [pltpu.VMEM(s, t) for s, t in scratch]
             + [
                 sem((8,)), sem((8,)), sem((8,)), sem((8,)), sem((2,)),
                 sem((max(half - 1, 1),)), sem((max(half - 1, 1),)),
@@ -553,11 +602,17 @@
                 collective_id=0, has_side_effects=True, vmem_limit_bytes=60 * 2**20
             ),
         )(inputs, upstream, weights, probe_init)
-        outputs, input_grad, kernel_grad, probe_out, scalars = outs
-        return (
-            outputs, input_grad, kernel_grad, probe_out,
-            scalars[0, 0], scalars[1:ITERS, 0],
-        )
+        smem = pl.BlockSpec(memory_space=pltpu.SMEM)
+        *arrays, lipschitz, norm_trace = pl.pallas_call(
+            finish,
+            out_shape=tuple(jax.ShapeDtypeStruct(x.shape, x.dtype) for x in outs[:4])
+            + (jax.ShapeDtypeStruct((1,), F32), jax.ShapeDtypeStruct((ITERS - 1,), F32)),
+            in_specs=[anywhere] * 4 + [smem],
+            out_specs=[anywhere] * 4 + [smem] * 2,
+            scratch_shapes=[sem((2 * batch + 2,))],
+            compiler_params=pltpu.CompilerParams(vmem_limit_bytes=60 * 2**20),
+        )(*outs)
+        return (*arrays, lipschitz.reshape(()), norm_trace)
 
     placed = (
         P("rep", "rows", "cols", None),

time: 57.3 us -> 134 us (2.34)
  Pallas kernels: 49.1 us -> 133 us
  local copies, waits for them, and re-layouts: 7.32 us -> 0 us
    pallas_call x0 -> x1, Pallas kernels: none -> 86.3 us  [per_device(): pl.pallas_call(finish, out_shape=tuple((jax.ShapeDtypeStruct(x.shape, x.d...]
    unnamed x10 -> x0, local copies, waits for them, and re-layouts: 4.75 us -> none
    slice x2 -> x0, local copies, waits for them, and re-layouts: 2.57 us -> none  [the longest x1 1.3 us: per_device(): scalars[1:ITERS, 0]]
    pallas_call x1, Pallas kernels: 49.1 us -> 46.6 us  [per_device(): pl.pallas_call(functools.partial(kernel, nr, nc, (cell_count, grad_scale)...]
where the time goes in v2:
time: 134 us
  Pallas kernels  133 us (99%)
    pallas_call x1, Pallas kernels, per_device(): pl.pallas_call(finish, out_shape=tuple((jax.ShapeDtypeStruct(x.shape, x.d...  86.3 us
    pallas_call x1, Pallas kernels, per_device(): pl.pallas_call(functools.partial(kernel, nr, nc, (cell_count, grad_scale)...  46.6 us

profile of v2, /device:TPU:0, one launch (start us, length us, event | category | flops | bytes accessed | tf_op | source)
XLA Modules:
  0.0 133.5 jit_solution(14024252945602530038)
XLA Ops:
  0.6 46.6 %shard_map.91 = (bf16[4,16,32,256]{3,2,1,0:T(8,128)(2,1)}, bf16[4,16,32,256]{3,2,1,0:T(8,128)(2,1)}, f32[16,2304]{1,0:T(8,128)}, f32[16,32,256]{2,1,0:T(8,128)}, f32[8,128]{1,0:T(8,128)}) custom-call(bf16[4,16,32,256]{3,2,1,0:T(8,128)(2,1)} %in_hbm.1, bf16[4,16,32,256]{3,2,1,0:T(8,128)(2,1)} %up_hbm.1, bf16[3,3,256,256]{3,2,1,0:T(8,128)(2,1)} %k_hbm.1, ...), custom_call_target="tpu_custom_call" | custom-call | tf_op jit(solution)/shard_map/pallas_call | solution.py:582
  47.2 86.3 %shard_map.92 = (bf16[4,16,32,256]{3,2,1,0:T(8,128)(2,1)}, bf16[4,16,32,256]{3,2,1,0:T(8,128)(2,1)}, f32[16,2304]{1,0:T(8,128)}, f32[16,32,256]{2,1,0:T(8,128)}, f32[1]{0:T(128)}, /*index=5*/f32[3]{0:T(128)}) custom-call(bf16[4,16,32,256]{3,2,1,0:T(8,128)(2,1)} %get-tuple-element.17.o_in, bf16[4,16,32,256]{3,2,1,0:T(8,128)(2,1)} %get-tuple-element.18.g_in, ...), custom_call_target="tpu_custom_call" | custom-call | tf_op jit(solution)/shard_map/pallas_call | solution.py:606

commit v3 on v2

--- a/solution.py
+++ b/solution.py
@@ -28,8 +28,8 @@
     in_ref, up_ref, k_ref, p_ref, o_ref, g_ref, load, store,
     fs_row, fr_row, fs_col, fr_col, fs_cor, fr_cor,
     pb, pr_row, ps_col, pr_col, ps_cor, pr_cor,
-    xin, xup, xa, xb, wt, ut, gb, r0, h1, r1, h2, r2, h3, r3, tab,
-    f_send, f_recv, p_send, p_recv, s0, s1s, s1r, s2s, s2r, s3, ts, tr,
+    xin, xup, xa, xb, wt, ut, gb, r0, h1, r1, h2, r2, h3, r3, tab, yh,
+    f_send, f_recv, p_send, p_recv, s0, s1s, s1r, s2s, s2r, s3, ts, tr, sa, sy,
 ):
     batch, height, breadth, ch = in_ref.shape
     halo = 2 * ITERS
@@ -49,6 +49,7 @@
         one.start()
     n = nr * nc
     half = nc // 2
+    own_rows = height // 2
     ri, ci, rp = lax.axis_index("rows"), lax.axis_index("cols"), lax.axis_index("rep")
     me = ri * nc + ci
     core, cy = lax.rem(ci, 2), ci // 2
@@ -85,13 +86,12 @@
                 ).astype(BF16)
     loads[2].wait()
     pb[...] = p_ref[...].astype(BF16)
+    sent_row = (height - halo) * (1 - rp)
     for h, col in ((0, 0), (1, breadth - halo)):
         edge = p_ref[:, col : col + halo, :]
         ps_col[h] = edge.reshape(height * halo // 16, 16, ch).astype(BF16)
-        for v, row in ((0, 0), (1, height - halo)):
-            ps_cor[v, h] = (
-                edge[row : row + halo].reshape(halo * halo // 16, 16, ch).astype(BF16)
-            )
+        edge = p_ref[pl.ds(sent_row, halo), col : col + halo, :]
+        ps_cor[h] = edge.reshape(halo * halo // 16, 16, ch).astype(BF16)
 
     pl.semaphore_wait(barrier, n)
 
@@ -128,17 +128,20 @@
         )
 
     def p_copy(k):
-        v, h = SIDES[k]
-        if h == 0:
-            src = pb.at[pl.ds(0 if v < 0 else height - halo, halo)]
+        h = (0, -1, 1, -1, 1)[k]
+        if k == 0:
+            src, dst = pb.at[pl.ds(sent_row, halo)], pr_row
+        elif k < 3:
+            src, dst = ps_cor.at[sidx(h)], pr_cor.at[sidx(-h)]
         else:
-            src = buffers(v, h, None, ps_col, ps_cor)
+            src, dst = ps_col.at[sidx(h)], pr_col.at[sidx(-h)]
+        row = lax.rem(ri + 1 - 2 * rp + nr, nr) if k < 3 else ri
         return pltpu.make_async_remote_copy(
             src_ref=src,
-            dst_ref=buffers(-v, -h, pr_row, pr_col, pr_cor),
+            dst_ref=dst,
             send_sem=p_send.at[k],
             recv_sem=p_recv.at[k],
-            device_id=target(v, h),
+            device_id=dev(row, lax.rem(ci + h + nc, nc), rp),
             device_id_type=MESH,
         )
 
@@ -152,7 +155,7 @@
             ref = buffers(v, h, fr_row, fr_col, fr_cor)
             ref[...] = jnp.zeros(ref.shape, BF16)
 
-    for k in range(8):
+    for k in range(5):
         p_copy(k).start()
 
     loads[3].wait()
@@ -267,7 +270,7 @@
 
     copy0().start()
 
-    def field_conv(src, dst, weights):
+    def field_conv(src, dst, weights, begin, end):
         block = min(height, 8)
 
         def step(t, c):
@@ -282,7 +285,9 @@
             dst[b, pl.ds(row, block)] = acc.reshape(block, breadth, ch).astype(BF16)
             return c
 
-        lax.fori_loop(0, batch * (height // block), step, 0)
+        lax.fori_loop(
+            begin * (height // block), end * (height // block), step, 0
+        )
 
     def forward():
         return k_ref[...].reshape(9 * ch, ch)
@@ -290,7 +295,7 @@
     def adjoint():
         return wt[...].reshape(9 * ch, ch)
 
-    field_conv(xin, o_ref, forward)
+    field_conv(xin, o_ref, forward, 0, batch)
     stores[0].start()
 
     copy0().wait_recv()
@@ -315,22 +320,21 @@
         dst[pl.ds(row, rows), :, ch : 2 * ch] = value.astype(BF16)
         dst[pl.ds(row, rows), :, 2 * ch :] = right.reshape(rows, wide, ch).astype(BF16)
 
-    for k in range(8):
+    for k in range(5):
         p_copy(k).wait_recv()
-    for s, row in ((0, 0), (1, height + halo)):
-        put(
-            xa, row,
-            jnp.concatenate(
-                [
-                    pr_cor[s, 0].astype(F32).reshape(halo, halo, ch),
-                    pr_row[s].astype(F32),
-                    pr_cor[s, 1].astype(F32).reshape(halo, halo, ch),
-                ],
-                axis=1,
-            ),
-        )
     put(
-        xa, halo,
+        xa, rp * height,
+        jnp.concatenate(
+            [
+                pr_cor[0].astype(F32).reshape(halo, halo, ch),
+                pr_row[...].astype(F32),
+                pr_cor[1].astype(F32).reshape(halo, halo, ch),
+            ],
+            axis=1,
+        ),
+    )
+    put(
+        xa, halo * (1 - rp),
         jnp.concatenate(
             [
                 pr_col[0].astype(F32).reshape(height, halo, ch),
@@ -356,10 +360,10 @@
         return jnp.sum(jnp.sum(x, axis=0, keepdims=True), axis=1, keepdims=True)
 
     def note(row, value):
-        tab[me, row : row + 1, :] = jnp.broadcast_to(value, (1, 128))
+        tab[me, rp, row : row + 1, :] = jnp.broadcast_to(value, (1, 128))
 
     factor = None
-    rows = height + 2 * halo
+    rows = own_rows + 2 * halo
     for it in range(ITERS):
         rows -= 2
         block = split_rows(rows)
@@ -374,7 +378,7 @@
         lax.fori_loop(0, rows // block, ahead, 0)
         rows -= 2
         block = split_rows(rows)
-        first = (rows - height) // 2
+        first = (rows - own_rows) // 2
         last = it + 1 == ITERS
 
         def back(t, c, block=block, first=first, last=last):
@@ -383,11 +387,11 @@
             full = acc.reshape(block, wide, ch)
             mine = full[:, halo : halo + breadth, :]
             if last:
-                po_ref[pl.ds(t * block, block)] = mine
+                yh[rp, pl.ds(t * block, block)] = mine.astype(BF16)
                 return own + fold(mine * mine), every, rounded
             put(xa, t * block, full)
             where = t * block + lax.broadcasted_iota(jnp.int32, mine.shape, 0)
-            inside = jnp.logical_and(where >= first, where < first + height)
+            inside = jnp.logical_and(where >= first, where < first + own_rows)
             mine = jnp.where(inside, mine, 0.0)
             near = mine.astype(BF16).astype(F32)
             return (
@@ -406,7 +410,7 @@
             root = jnp.sqrt(jnp.maximum(mean, 1e-30))
             factor = 1.0 / root
             note(ITERS + 1 + it, root)
-        if it == 0:
+        if it == 1:
             for k in range(1, half):
                 copy1(k).wait_recv()
 
@@ -420,14 +424,28 @@
             lax.fori_loop(0, nr, sum1, 0)
             for k in range(1, nr):
                 copy2(k).start()
-        if it == ITERS - 2:
-            for k in range(1, nr):
-                copy2(k).wait_recv()
-            acc = h2[ri].astype(F32)
-            for k in range(1, nr):
-                acc = acc + r2[k - 1].astype(F32)
-            h3[...] = acc
-            copy3().start()
+    def copya():
+        return pltpu.make_async_remote_copy(
+            src_ref=tab.at[me, rp],
+            dst_ref=tab.at[me, rp],
+            send_sem=sa.at[0],
+            recv_sem=sa.at[1],
+            device_id=dev(ri, ci, 1 - rp),
+            device_id_type=MESH,
+        )
+
+    def copyy():
+        return pltpu.make_async_remote_copy(
+            src_ref=yh.at[rp],
+            dst_ref=yh.at[rp],
+            send_sem=sy.at[0],
+            recv_sem=sy.at[1],
+            device_id=dev(ri, ci, 1 - rp),
+            device_id_type=MESH,
+        )
+
+    copya().start()
+    copyy().start()
 
     def copyt(k):
         to = lax.rem(me + k, n)
@@ -455,9 +473,17 @@
         copyt(k).start()
         return c
 
+    field_conv(xup, g_ref, adjoint, 0, batch // 2)
+    copya().wait_recv()
     lax.fori_loop(1, n, tell, 0)
-
-    field_conv(xup, g_ref, adjoint)
+    for k in range(1, nr):
+        copy2(k).wait_recv()
+    acc = h2[ri].astype(F32)
+    for k in range(1, nr):
+        acc = acc + r2[k - 1].astype(F32)
+    h3[...] = acc.astype(BF16)
+    copy3().start()
+    field_conv(xup, g_ref, adjoint, batch // 2, batch)
     stores[1].start()
 
     def hear(k, c):
@@ -465,8 +491,8 @@
         return c
 
     lax.fori_loop(1, n, hear, 0)
-    told = tab[...]
-    gain = jnp.ones((n, 128), F32)
+    told = tab[...].reshape(2 * n, 8, 128)
+    gain = jnp.ones((2 * n, 128), F32)
     for it in range(ITERS - 1):
         squared = jnp.sum(told[:, it, :] * gain * gain, axis=0, keepdims=True)
         scale = jnp.sqrt(squared / cell_count + 1e-06)
@@ -477,22 +503,27 @@
         gain = gain * told[:, ITERS + 1 + it, :]
     sum_back = jnp.sum(told[:, ITERS - 1, :] * gain * gain, axis=0, keepdims=True)
     sc_ref[0:1, :] = jnp.sqrt(jnp.sqrt(sum_back / sum_probe))
-    own_gain = 1.0 / jnp.sqrt(sum_back / cell_count + 1e-06)
-    for it in range(ITERS - 1):
-        own_gain = own_gain * tab[me, ITERS + 1 + it : ITERS + 2 + it, :]
-        own_gain = own_gain / sc_ref[it + 1 : it + 2, :]
-    both = jnp.concatenate([own_gain] * (ch // 128), axis=1).reshape(1, 1, ch)
-    po_ref[...] = po_ref[...] * both
+    copyy().wait_recv()
+    for q in range(2):
+        own_gain = 1.0 / jnp.sqrt(sum_back / cell_count + 1e-06)
+        for it in range(ITERS - 1):
+            own_gain = own_gain * tab[me, q, ITERS + 1 + it : ITERS + 2 + it, :]
+            own_gain = own_gain / sc_ref[it + 1 : it + 2, :]
+        both = jnp.concatenate([own_gain] * (ch // 128), axis=1).reshape(1, 1, ch)
+        po_ref[q * own_rows : (q + 1) * own_rows] = yh[q].astype(F32) * both
 
     copy3().wait_recv()
-    kg_ref[...] = (h3[...] + r3[...]) * grad_scale
+    kg_ref[...] = (h3[...].astype(F32) + r3[...].astype(F32)) * grad_scale
 
     for k, (v, h) in enumerate(SIDES):
         @pl.when(exists(v, h))
         def _(k=k):
             f_copy(k).wait_send()
 
+    for k in range(5):
         p_copy(k).wait_send()
+    copya().wait_send()
+    copyy().wait_send()
     copy0().wait_send()
     for k in range(1, half):
         copy1(k).wait_send()
@@ -510,23 +541,32 @@
     lax.fori_loop(1, n, sent, 0)
 
 
-def finish(o_in, g_in, kg_in, po_in, sc_in, o_out, g_out, kg_out, po_out, lip, trace, sems):
-    copies = []
+def finish(
+    o_in, g_in, kg_in, po_in, sc_in, o_out, g_out, kg_out, po_out, lip, trace,
+    o_mid, g_mid, kg_mid, po_mid, in_sems, out_sems,
+):
+    parts = []
     for a in range(o_in.shape[0]):
-        copies.append((o_in.at[a], o_out.at[a]))
-        copies.append((g_in.at[a], g_out.at[a]))
-    copies.append((po_in, po_out))
-    copies.append((kg_in, kg_out))
-    started = [
-        pltpu.make_async_copy(src, dst, sems.at[i]) for i, (src, dst) in enumerate(copies)
+        parts.append((o_in.at[a], o_mid.at[a], o_out.at[a]))
+        parts.append((g_in.at[a], g_mid.at[a], g_out.at[a]))
+    parts.append((po_in, po_mid, po_out))
+    parts.append((kg_in, kg_mid, kg_out))
+    inward = [
+        pltpu.make_async_copy(src, mid, in_sems.at[i]) for i, (src, mid, _) in enumerate(parts)
     ]
-    for one in started:
+    outward = [
+        pltpu.make_async_copy(mid, dst, out_sems.at[i]) for i, (_, mid, dst) in enumerate(parts)
+    ]
+    for one in inward:
         one.start()
     lip[0] = sc_in[0, 0]
     for i in range(ITERS - 1):
         trace[i] = sc_in[i + 1, 0]
-    for one in started:
+    for one, two in zip(inward, outward):
         one.wait()
+        two.start()
+    for two in outward:
+        two.wait()
 
 
 def solution(mesh):
@@ -553,15 +593,15 @@
             ((2, 2, 2 * batch, 16, ch), BF16),
             ((2, 2, 2 * batch, 16, ch), BF16),
             ((height, breadth, ch), BF16),
-            ((2, halo, breadth, ch), BF16),
+            ((halo, breadth, ch), BF16),
             ((2, height * halo // 16, 16, ch), BF16),
             ((2, height * halo // 16, 16, ch), BF16),
-            ((2, 2, halo * halo // 16, 16, ch), BF16),
-            ((2, 2, halo * halo // 16, 16, ch), BF16),
+            ((2, halo * halo // 16, 16, ch), BF16),
+            ((2, halo * halo // 16, 16, ch), BF16),
             ((batch, height + 2, breadth, 3 * ch), BF16),
             ((batch, height + 2, breadth, 3 * ch), BF16),
-            ((height + 2 * halo, wide, 3 * ch), BF16),
-            ((height + 2 * halo, wide, 3 * ch), BF16),
+            ((height + halo, wide, 3 * ch), BF16),
+            ((height + halo, wide, 3 * ch), BF16),
             ((3, 3 * ch, ch), BF16),
             ((ch, batch * cells), BF16),
             ((2, half, nr, dper, 9 * ch), BF16),
@@ -570,9 +610,10 @@
             ((half - 1, nr, dper, 9 * ch), BF16),
             ((nr, dper, 9 * ch), BF16),
             ((nr - 1, dper, 9 * ch), BF16),
-            ((dper, 9 * ch), F32),
-            ((dper, 9 * ch), F32),
-            ((n, 8, 128), F32),
+            ((dper, 9 * ch), BF16),
+            ((dper, 9 * ch), BF16),
+            ((n, 2, 8, 128), F32),
+            ((2, height // 2, breadth, ch), BF16),
         ]
         anywhere = pl.BlockSpec(memory_space=pl.ANY)
         staged = [
@@ -594,9 +635,10 @@
             + [sem((4,)), sem((2,))]
             + [pltpu.VMEM(s, t) for s, t in scratch]
             + [
-                sem((8,)), sem((8,)), sem((8,)), sem((8,)), sem((2,)),
+                sem((8,)), sem((8,)), sem((5,)), sem((5,)), sem((2,)),
                 sem((max(half - 1, 1),)), sem((max(half - 1, 1),)),
                 sem((nr - 1,)), sem((nr - 1,)), sem((2,)), sem((n,)), sem((n,)),
+                sem((2,)), sem((2,)),
             ],
             compiler_params=pltpu.CompilerParams(
                 collective_id=0, has_side_effects=True, vmem_limit_bytes=60 * 2**20
@@ -609,7 +651,8 @@
             + (jax.ShapeDtypeStruct((1,), F32), jax.ShapeDtypeStruct((ITERS - 1,), F32)),
             in_specs=[anywhere] * 4 + [smem],
             out_specs=[anywhere] * 4 + [smem] * 2,
-            scratch_shapes=[sem((2 * batch + 2,))],
+            scratch_shapes=[pltpu.VMEM(x.shape, x.dtype) for x in outs[:4]]
+            + [sem((2 * batch + 2,)), sem((2 * batch + 2,))],
             compiler_params=pltpu.CompilerParams(vmem_limit_bytes=60 * 2**20),
         )(*outs)
         return (*arrays, lipschitz.reshape(()), norm_trace)

time: 134 us -> 47.4 us (0.35)
  Pallas kernels: 133 us -> 46.5 us
    pallas_call x1, Pallas kernels: 86.3 us -> 3.93 us  [per_device(): pl.pallas_call(finish, out_shape=tuple((jax.ShapeDtypeStruct(x.shape, x.d...]
    pallas_call x1, Pallas kernels: 46.6 us -> 42.6 us  [per_device(): pl.pallas_call(functools.partial(kernel, nr, nc, (cell_count, grad_scale)...]
where the time goes in v3:
time: 47.4 us; the launch traced here: 47.2 us
  Pallas kernels  46.5 us (98%)
  between operations  0.64 us (1%)
    pallas_call x1, Pallas kernels, per_device(): pl.pallas_call(functools.partial(kernel, nr, nc, (cell_count, grad_scale)...  42.6 us
    pallas_call x1, Pallas kernels, per_device(): pl.pallas_call(finish, out_shape=tuple((jax.ShapeDtypeStruct(x.shape, x.d...  3.93 us

profile of v3, /device:TPU:0, one launch (start us, length us, event | category | flops | bytes accessed | tf_op | source)
XLA Modules:
  0.0 47.2 jit_solution(7425622797140946907)
XLA Ops:
  0.6 42.6 %shard_map.91 = (bf16[4,16,32,256]{3,2,1,0:T(8,128)(2,1)}, bf16[4,16,32,256]{3,2,1,0:T(8,128)(2,1)}, f32[16,2304]{1,0:T(8,128)}, f32[16,32,256]{2,1,0:T(8,128)}, f32[8,128]{1,0:T(8,128)}) custom-call(bf16[4,16,32,256]{3,2,1,0:T(8,128)(2,1)} %in_hbm.1, bf16[4,16,32,256]{3,2,1,0:T(8,128)(2,1)} %up_hbm.1, bf16[3,3,256,256]{3,2,1,0:T(8,128)(2,1)} %k_hbm.1, ...), custom_call_target="tpu_custom_call" | custom-call | tf_op jit(solution)/shard_map/pallas_call | solution.py:623
  43.2 3.9 %shard_map.92 = (bf16[4,16,32,256]{3,2,1,0:T(8,128)(2,1)}, bf16[4,16,32,256]{3,2,1,0:T(8,128)(2,1)}, f32[16,2304]{1,0:T(8,128)}, f32[16,32,256]{2,1,0:T(8,128)}, f32[1]{0:T(128)}, /*index=5*/f32[3]{0:T(128)}) custom-call(bf16[4,16,32,256]{3,2,1,0:T(8,128)(2,1)} %get-tuple-element.17.o_in, bf16[4,16,32,256]{3,2,1,0:T(8,128)(2,1)} %get-tuple-element.18.g_in, ...), custom_call_target="tpu_custom_call" | custom-call | tf_op jit(solution)/shard_map/pallas_call | solution.py:648

commit v4 on v3

--- a/solution.py
+++ b/solution.py
@@ -295,8 +295,7 @@
     def adjoint():
         return wt[...].reshape(9 * ch, ch)
 
-    field_conv(xin, o_ref, forward, 0, batch)
-    stores[0].start()
+    field_conv(xin, o_ref, forward, 0, 1)
 
     copy0().wait_recv()
 
@@ -309,6 +308,8 @@
     for k in range(1, half):
         copy1(k).start()
 
+    field_conv(xin, o_ref, forward, 1, batch)
+    stores[0].start()
     pad_fields(1, up_ref, xup)
 
     def put(dst, row, value):
@@ -410,7 +411,7 @@
             root = jnp.sqrt(jnp.maximum(mean, 1e-30))
             factor = 1.0 / root
             note(ITERS + 1 + it, root)
-        if it == 1:
+        if it == 0:
             for k in range(1, half):
                 copy1(k).wait_recv()
 
@@ -473,7 +474,7 @@
         copyt(k).start()
         return c
 
-    field_conv(xup, g_ref, adjoint, 0, batch // 2)
+    field_conv(xup, g_ref, adjoint, 0, 1)
     copya().wait_recv()
     lax.fori_loop(1, n, tell, 0)
     for k in range(1, nr):
@@ -483,7 +484,7 @@
         acc = acc + r2[k - 1].astype(F32)
     h3[...] = acc.astype(BF16)
     copy3().start()
-    field_conv(xup, g_ref, adjoint, batch // 2, batch)
+    field_conv(xup, g_ref, adjoint, 1, batch)
     stores[1].start()
 
     def hear(k, c):

time: 47.4 us -> 48.4 us (1.021)
  Pallas kernels: 46.5 us -> 47.6 us
    pallas_call x1, Pallas kernels: 42.6 us -> 43.6 us  [per_device(): pl.pallas_call(functools.partial(kernel, nr, nc, (cell_count, grad_scale)...]
where the time goes in v4:
time: 48.4 us; the launch traced here: 48.2 us
  Pallas kernels  47.6 us (98%)
  between operations  0.64 us (1%)
    pallas_call x1, Pallas kernels, per_device(): pl.pallas_call(functools.partial(kernel, nr, nc, (cell_count, grad_scale)...  43.6 us
    pallas_call x1, Pallas kernels, per_device(): pl.pallas_call(finish, out_shape=tuple((jax.ShapeDtypeStruct(x.shape, x.d...  3.93 us

profile of v4, /device:TPU:0, one launch (start us, length us, event | category | flops | bytes accessed | tf_op | source)
XLA Modules:
  0.0 48.2 jit_solution(7345144424385694653)
XLA Ops:
  0.6 43.6 %shard_map.91 = (bf16[4,16,32,256]{3,2,1,0:T(8,128)(2,1)}, bf16[4,16,32,256]{3,2,1,0:T(8,128)(2,1)}, f32[16,2304]{1,0:T(8,128)}, f32[16,32,256]{2,1,0:T(8,128)}, f32[8,128]{1,0:T(8,128)}) custom-call(bf16[4,16,32,256]{3,2,1,0:T(8,128)(2,1)} %in_hbm.1, bf16[4,16,32,256]{3,2,1,0:T(8,128)(2,1)} %up_hbm.1, bf16[3,3,256,256]{3,2,1,0:T(8,128)(2,1)} %k_hbm.1, ...), custom_call_target="tpu_custom_call" | custom-call | tf_op jit(solution)/shard_map/pallas_call | solution.py:624
  44.3 3.9 %shard_map.92 = (bf16[4,16,32,256]{3,2,1,0:T(8,128)(2,1)}, bf16[4,16,32,256]{3,2,1,0:T(8,128)(2,1)}, f32[16,2304]{1,0:T(8,128)}, f32[16,32,256]{2,1,0:T(8,128)}, f32[1]{0:T(128)}, /*index=5*/f32[3]{0:T(128)}) custom-call(bf16[4,16,32,256]{3,2,1,0:T(8,128)(2,1)} %get-tuple-element.17.o_in, bf16[4,16,32,256]{3,2,1,0:T(8,128)(2,1)} %get-tuple-element.18.g_in, ...), custom_call_target="tpu_custom_call" | custom-call | tf_op jit(solution)/shard_map/pallas_call | solution.py:649
